TPU v7x, 32 devices: a whole 2x2x4 slice. The times are simulated.
32 devices in a mesh: dist: 4 (over x, core), ctr: 8 (over z, y).
Axes of the slice: x: 2, y: 2, z: 4, core: 2. Of those that a mesh axis runs over, the one named last changes fastest.
Arguments:
- three_centre: bfloat16 [1024, 4, 4096], P(('dist', 'ctr')), may hold values from -0.359375 to 0.359375
- occupied_green: bfloat16 [128, 4096], P(('dist', 'ctr')), may hold values from -0.75 to 0.75
- virtual_green: bfloat16 [128, 4096], P(('dist', 'ctr')), may hold values from -0.75 to 0.75
- pair_index: int32 [16, 4], replicated, may hold values from 0 to 7, as said below
- source_slot: int32 [16, 4, 4], replicated, may hold values from -1 to 3, as said below
- occupied_index: int32 [16, 4, 4], replicated, may hold values from 0 to 127, as said below
- virtual_index: int32 [16, 4, 4], replicated, may hold values from 0 to 127, as said below
Outputs:
- density_response: float32 [1024, 256], P(('dist', 'ctr'))
Inputs may be any that keep to these rules, and one draw needn't show every extreme that they name: `pair_index`: the 4 entries of a row are distinct. `source_slot`: for each slot the listed slots are distinct and come first, followed by -1 entries; all slots of one auxiliary atom list the same number of slots, at least 1; in every draw some auxiliary atom lists 4. `occupied_index`: for auxiliary atom p with g = p // 4, every entry lies in g * 32 to g * 32 + 2 * 32 - 1, taken modulo 128. `virtual_index`: for auxiliary atom p with g = p // 4, every entry lies in g * 32 to g * 32 + 2 * 32 - 1, taken modulo 128.
All inputs are finite; a program needn't handle non-finite values.
Results may differ from a plain program's by a relative error of at most 0.004.
Values may be sent and summed in bfloat16 or wider, within the bound.
A program may use at most 64 MiB of HBM per device.

v0:
```python
import jax
import jax.numpy as jnp
from jax import lax
from jax.sharding import PartitionSpec as P

BLK = 64
AUXB = 64
NPR = 8


def shifted(block, axis, distance):
    devices = range(lax.axis_size(axis))
    route = [((i - distance) % len(devices), i) for i in devices]
    return lax.ppermute(block, axis, route)


def shards(
    three_centre,
    occupied_green,
    virtual_green,
    pair_index,
    source_slot,
    occupied_index,
    virtual_index,
):
    row_count = three_centre.shape[0]
    slot_count = three_centre.shape[1]
    ctr_size = lax.axis_size("ctr")
    dist_size = lax.axis_size("dist")
    dist_index = lax.axis_index("dist")
    ctr_index = lax.axis_index("ctr")
    flat_index = dist_index * ctr_size + ctr_index
    atom_index = flat_index * row_count // AUXB
    source_rows = lax.dynamic_index_in_dim(source_slot, atom_index, 0, keepdims=False)
    occ_ids = lax.dynamic_index_in_dim(occupied_index, atom_index, 0, keepdims=False)
    virt_ids = lax.dynamic_index_in_dim(virtual_index, atom_index, 0, keepdims=False)
    occ_own, virt_own = (
        lax.all_gather(occupied_green, "ctr", axis=0, tiled=True),
        lax.all_gather(virtual_green, "ctr", axis=0, tiled=True),
    )
    following = shifted(jnp.stack([occ_own, virt_own]), "dist", -1)
    occ_table = jnp.concatenate([occ_own, following[0]], axis=0)
    virt_table = jnp.concatenate([virt_own, following[1]], axis=0)
    region_base = dist_index * occ_own.shape[0]
    list_total = occ_own.shape[0] * dist_size
    occ_position = jnp.mod(occ_ids - region_base, list_total)
    virt_position = jnp.mod(virt_ids - region_base, list_total)
    tensor_rows = three_centre.reshape(row_count, slot_count, BLK, BLK)
    accumulated = jnp.zeros(tensor_rows.shape, jnp.float32)
    for step in range(source_rows.shape[1]):
        source_col = source_rows[:, step]
        live_mask = (source_col >= 0).astype(jnp.float32)
        picked = jnp.take(tensor_rows, jnp.maximum(source_col, 0), axis=1)
        virt_blocks = jnp.take(virt_table, virt_position[:, step], axis=0).reshape(
            slot_count, BLK, BLK
        )
        product = jnp.einsum(
            "aslv,svz->aslz", picked, virt_blocks, preferred_element_type=jnp.float32
        )
        product = (product * live_mask[None, :, None, None]).astype(jnp.bfloat16)
        occ_blocks = jnp.take(occ_table, occ_position[:, step], axis=0).reshape(
            slot_count, BLK, BLK
        )
        accumulated = accumulated + jnp.einsum(
            "slm,aslz->asmz", occ_blocks, product, preferred_element_type=jnp.float32
        )
    updated = accumulated.astype(jnp.bfloat16).reshape(row_count, slot_count, BLK * BLK)
    upd_region, ten_region = (
        lax.all_to_all(updated, "ctr", split_axis=2, concat_axis=0, tiled=True),
        lax.all_to_all(three_centre, "ctr", split_axis=2, concat_axis=0, tiled=True),
    )
    region_rows = upd_region.shape[0]
    col_count = upd_region.shape[2]
    region_atoms = region_rows // AUXB
    region_pairs = lax.dynamic_slice_in_dim(pair_index, dist_index * region_atoms, region_atoms, 0)
    one_hot = (region_pairs[:, :, None] == jnp.arange(NPR)[None, None, :]).astype(jnp.bfloat16)
    upd_blocks = upd_region.reshape(region_atoms, AUXB, slot_count, col_count)
    ten_blocks = ten_region.reshape(region_atoms, AUXB, slot_count, col_count)
    upd_space = (
        jnp.einsum("psk,pasc->kpac", one_hot, upd_blocks, preferred_element_type=jnp.float32)
        .astype(jnp.bfloat16)
        .reshape(NPR, region_rows, col_count)
    )
    ten_space = (
        jnp.einsum("psk,pasc->kpac", one_hot, ten_blocks, preferred_element_type=jnp.float32)
        .astype(jnp.bfloat16)
        .reshape(NPR, region_rows, col_count)
    )
    return lax.psum_scatter(
        jnp.einsum("kac,kbc->ab", upd_space, ten_space, preferred_element_type=jnp.float32),
        "ctr",
        scatter_dimension=0,
        tiled=True,
    )


def solution(mesh):
    return jax.shard_map(
        shards,
        mesh=mesh,
        in_specs=(
            P(("dist", "ctr"), None, None),
            P(("dist", "ctr"), None),
            P(("dist", "ctr"), None),
            P(),
            P(),
            P(),
            P(),
        ),
        out_specs=P(("dist", "ctr"), None),
        check_vma=False,
    )
```

profile of v0, /device:TPU:0, one launch (start us, length us, event | category | flops | bytes accessed | tf_op | source)
XLA Modules:
  0.0 265.6 jit_solution(9622120785204081876)
XLA Ops:
  6.5 32.9 %all-gather.1 = bf16[8,4,4096]{2,1,0:T(4,128)(2,1)S(1)} all-gather(bf16[1,4,4096]{2,1,0:T(4,128)(2,1)} %bitcast.126), channel_id=1, replica_groups=mesh['dist'=4,'ctr'=8] {'ctr'}, dimensions={0}, use_global_device_ids=true | all-gather | bytes 294912 | tf_op jit(solution)/shard_map/all_gather | solution.py:38
  39.4 30.9 %all-gather = bf16[8,4,4096]{2,1,0:T(4,128)(2,1)S(1)} all-gather(bf16[1,4,4096]{2,1,0:T(4,128)(2,1)} %bitcast.127), channel_id=1, replica_groups=mesh['dist'=4,'ctr'=8] {'ctr'}, dimensions={0}, use_global_device_ids=true | all-gather | bytes 294912 | tf_op jit(solution)/shard_map/all_gather | solution.py:39
  70.5 0.8 pad_maximum_fusion
  71.3 4.8 %copy.40 = bf16[32,4,4096]{0,1,2:T(4,128)(2,1)} copy(bf16[32,4,4096]{2,1,0:T(4,128)(2,1)S(1)} %copy-done.3) | data formatting | bytes 2097152 | tf_op args[0]
  76.2 7.8 %reshape.296 = bf16[8,2,32768]{2,1,0:T(2,128)(2,1)} reshape(bf16[4096,4,32]{2,1,0:T(4,128)(2,1)} %bitcast.120) | data formatting | bytes 2097152
  84.0 5.7 %all-to-all-start.1 = ((bf16[8,2,32768]{2,1,0:T(2,128)(2,1)}), bf16[8,2,32768]{2,1,0:T(2,128)(2,1)}, u32[]{:S(2)}, u32[]{:S(2)}) async-start(bf16[8,2,32768]{2,1,0:T(2,128)(2,1)} %reshape.296), calls=%async_computation.1 | async-start | bytes 2097152 | tf_op jit(solution)/shard_map/all_to_all | solution.py:70
  91.4 0.8 reshape.236
  92.2 1.8 reshape.108
  94.3 2.2 gather_fusion.10
  96.4 2.2 gather_fusion.7
  98.6 2.2 gather_fusion.4
  100.8 2.1 gather_fusion.1
  103.0 1.1 slice_bitcast_fusion
  104.0 1.0 pad_maximum_fusion.1
  105.1 0.6 gather_fusion.9
  111.5 4.7 %fusion.2 = f32[4,32,64,64]{3,2,1,0:T(8,128)} fusion(bf16[4,32,64,64]{3,2,1,0:T(8,128)(2,1)S(1)} %copy-done.2, f32[4]{0:T(128)S(1)} %get-tuple-element.18, pred[4]{0:T(512)(128)(4,1)S(1)} %get-tuple-element.41, bf16[4,64,64]{2,1,0:T(8,128)(2,1)S(1)} %reshape.112, bf16[4,64,64,1]{2,1,0,3:T(8,128)(2,1)S(1)} %reshape.268), kind=kOutput, calls=%fused_computation.19 | convolution fusion | flops 135790592 | bytes 3211284 | tf_op jit(solution)/shard_map/slm,aslz->asmz/dot_general | solution.py:64
  116.2 6.5 %fusion.8 = f32[4,32,64,64]{3,2,1,0:T(8,128)} fusion(bf16[4,32,64,64]{3,2,1,0:T(8,128)(2,1)} %gather_fusion.1, f32[4]{0:T(128)S(1)} %get-tuple-element.16, pred[4]{0:T(512)(128)(4,1)S(1)} %get-tuple-element.47, bf16[4,64,64]{2,1,0:T(8,128)(2,1)S(1)} %reshape.107, bf16[4,64,64,1]{2,1,0,3:T(8,128)(2,1)S(1)} %reshape.264), kind=kOutput, calls=%fused_computation.25 | convolution fusion | flops 135790592 | bytes 3211284 | tf_op jit(solution)/shard_map/slm,aslz->asmz/dot_general | solution.py:64
  122.6 4.7 %fusion.5 = f32[4,32,64,64]{3,2,1,0:T(8,128)} fusion(bf16[4,32,64,64]{3,2,1,0:T(8,128)(2,1)S(1)} %copy-done.1, f32[4]{0:T(128)S(1)} %get-tuple-element.17, pred[4]{0:T(512)(128)(4,1)S(1)} %get-tuple-element.44, bf16[4,64,64]{2,1,0:T(8,128)(2,1)S(1)} %reshape.110, bf16[4,64,64,1]{2,1,0,3:T(8,128)(2,1)S(1)} %reshape.266), kind=kOutput, calls=%fused_computation.22 | convolution fusion | flops 135790592 | bytes 3211284 | tf_op jit(solution)/shard_map/slm,aslz->asmz/dot_general | solution.py:64
  127.4 8.2 %fusion.22 = bf16[32,4,64,64]{2,3,0,1:T(8,128)(2,1)S(1)} fusion(f32[4,32,64,64]{3,2,1,0:T(8,128)} %fusion.2, f32[4,32,64,64]{3,2,1,0:T(8,128)} %fusion.8, f32[4,32,64,64]{3,2,1,0:T(8,128)} %fusion.5, bf16[4,32,64,64]{3,2,1,0:T(8,128)(2,1)} %gather_fusion.10, f32[4]{0:T(128)S(1)} %get-tuple-element.15, pred[4]{0:T(512)(128)(4,1)S(1)} %get-tuple-element.38, ...), kind=kOutput, calls=%fused_computation.41 | convolution fusion | flops 137887744 | bytes 8454164 | tf_op jit(solution)/shard_map/slm,aslz->asmz/dot_general | solution.py:64
  135.6 7.8 %copy.61 = bf16[32,4,64,64]{0,1,3,2:T(4,128)(2,1)} copy(bf16[32,4,64,64]{2,3,0,1:T(8,128)(2,1)S(1)} %fusion.22) | data formatting | bytes 2097152 | tf_op jit(solution)/shard_map/reshape | solution.py:67
  143.4 7.8 %reshape.298 = bf16[8,2,32768]{2,1,0:T(2,128)(2,1)} reshape(bf16[4096,4,32]{2,1,0:T(4,128)(2,1)} %bitcast.117) | data formatting | bytes 2097152
  151.2 6.1 %all-to-all-start = ((bf16[8,2,32768]{2,1,0:T(2,128)(2,1)}), bf16[8,2,32768]{2,1,0:T(2,128)(2,1)S(1)}, u32[]{:S(2)}, u32[]{:S(2)}) async-start(bf16[8,2,32768]{2,1,0:T(2,128)(2,1)} %reshape.298), calls=%async_computation | async-start | bytes 2097152 | tf_op jit(solution)/shard_map/all_to_all | solution.py:69
  157.6 7.0 %reshape.297 = bf16[4096,4,32]{2,1,0:T(4,128)(2,1)} reshape(bf16[8,2,32768]{2,1,0:T(2,128)(2,1)} %all-to-all-done.1) | data formatting | bytes 2097152
  164.6 6.1 %copy.41 = bf16[32,4,8,512]{3,1,0,2:T(4,128)(2,1)S(1)} copy(bf16[32,4,8,512]{0,1,3,2:T(4,128)(2,1)} %bitcast.118) | data formatting | bytes 2097152 | tf_op jit(solution)/shard_map/all_to_all | solution.py:70
  170.8 2.2 convolution_convert_fusion
  173.0 10.2 %all-to-all-done = bf16[8,2,32768]{2,1,0:T(2,128)(2,1)S(1)} async-done(((bf16[8,2,32768]{2,1,0:T(2,128)(2,1)}), bf16[8,2,32768]{2,1,0:T(2,128)(2,1)S(1)}, u32[]{:S(2)}, u32[]{:S(2)}) %all-to-all-start) | async-done | bytes 1048608 | tf_op jit(solution)/shard_map/all_to_all | solution.py:69
  183.2 4.5 %reshape.299 = bf16[4096,4,32]{2,1,0:T(4,128)(2,1)} reshape(bf16[8,2,32768]{2,1,0:T(2,128)(2,1)S(1)} %all-to-all-done) | data formatting | bytes 2097152
  187.8 4.7 %copy.62 = bf16[32,4,8,512]{3,2,0,1:T(8,128)(2,1)S(1)} copy(bf16[32,4,8,512]{0,1,3,2:T(4,128)(2,1)} %bitcast.119) | data formatting | bytes 2097152 | tf_op jit(solution)/shard_map/all_to_all | solution.py:69
  192.4 0.8 copy.38
  193.3 1.0 convolution_convert_fusion.1
  194.9 3.0 %fusion.41 = f32[256,256]{1,0:T(8,128)} fusion(bf16[8,256,512]{2,0,1:T(8,128)(2,1)S(1)} %bitcast.124, bf16[8,256,512]{2,0,1:T(8,128)(2,1)S(1)} %bitcast.125), kind=kOutput, calls=%fused_computation.42 | convolution fusion | flops 536870912 | bytes 4456448 | tf_op jit(solution)/shard_map/kac,kbc->ab/dot_general | solution.py:90
  197.9 60.9 %reduce-scatter.2.cloned.1.call-done = f32[32,256]{1,0:T(8,128)} async-done(((f32[256,256]{1,0:T(8,128)}), f32[32,256]{1,0:T(8,128)}) %reduce-scatter.2.cloned.1.call-update) | async-done | bytes 32784 | tf_op jit(solution)/shard_map/reduce_scatter | solution.py:89
  (82 shorter events, 8.4 us)
Async XLA Ops:
  6.5 83.2 %copy-start = (s32[16,4,4]{0,2,1:T(4,128)S(1)}, s32[16,4,4]{0,2,1:T(4,128)}, u32[]{:S(2)}) copy-start(s32[16,4,4]{0,2,1:T(4,128)} %param.15) | copy-start | bytes 3076
  6.5 64.8 %copy-start.3 = (bf16[32,4,4096]{2,1,0:T(4,128)(2,1)S(1)}, bf16[32,4,4096]{2,1,0:T(4,128)(2,1)}, u32[]{:S(2)}) copy-start(bf16[32,4,4096]{2,1,0:T(4,128)(2,1)} %param.11) | copy-start | bytes 3145732
  71.3 31.6 %collective-permute-start = (bf16[2,32,4096]{2,1,0:T(8,128)(2,1)}, bf16[2,32,4096]{2,1,0:T(8,128)(2,1)}, u32[]{:S(2)}, u32[]{:S(2)}) collective-permute-start(bf16[2,32,4096]{2,1,0:T(8,128)(2,1)} %pad_maximum_fusion), channel_id=1, source_target_pairs={{8,0},{16,8},{24,16},{0,24},{9,1},{17,9},{25,17},{1,25},{10,2},{18... | collective-permute-start | bytes 1572872 | tf_op jit(solution)/shard_map/ppermute | solution.py:14
  84.0 6.3 %copy-start.5 = (s32[16,4,4]{0,2,1:T(4,128)S(1)}, s32[16,4,4]{0,2,1:T(4,128)}, u32[]{:S(2)}) copy-start(s32[16,4,4]{0,2,1:T(4,128)} %param.16) | copy-start | bytes 3076
  84.0 6.8 %copy-start.6 = (s32[16,4,4]{0,2,1:T(4,128)S(1)}, s32[16,4,4]{0,2,1:T(4,128)}, u32[]{:S(2)}) copy-start(s32[16,4,4]{0,2,1:T(4,128)} %param.17) | copy-start | bytes 3076
  84.0 67.2 %all-to-all-start.1 = ((bf16[8,2,32768]{2,1,0:T(2,128)(2,1)}), bf16[8,2,32768]{2,1,0:T(2,128)(2,1)}, u32[]{:S(2)}, u32[]{:S(2)}) async-start(bf16[8,2,32768]{2,1,0:T(2,128)(2,1)} %reshape.296), calls=%async_computation.1 | async-start | bytes 2097152 | tf_op jit(solution)/shard_map/all_to_all | solution.py:70
  105.1 6.4 %copy-start.2 = (bf16[4,32,64,64]{3,2,1,0:T(8,128)(2,1)S(1)}, bf16[4,32,64,64]{3,2,1,0:T(8,128)(2,1)}, u32[]{:S(2)}) copy-start(bf16[4,32,64,64]{3,2,1,0:T(8,128)(2,1)} %gather_fusion.7) | copy-start | bytes 3145732
  116.2 6.5 %copy-start.1 = (bf16[4,32,64,64]{3,2,1,0:T(8,128)(2,1)S(1)}, bf16[4,32,64,64]{3,2,1,0:T(8,128)(2,1)}, u32[]{:S(2)}) copy-start(bf16[4,32,64,64]{3,2,1,0:T(8,128)(2,1)} %gather_fusion.4) | copy-start | bytes 3145732
  151.2 6.2 %copy-start.7 = (s32[16,4]{0,1:T(4,128)S(1)}, s32[16,4]{0,1:T(4,128)}, u32[]{:S(2)}) copy-start(s32[16,4]{0,1:T(4,128)} %param.14) | copy-start | bytes 772
  151.2 32.0 %all-to-all-start = ((bf16[8,2,32768]{2,1,0:T(2,128)(2,1)}), bf16[8,2,32768]{2,1,0:T(2,128)(2,1)S(1)}, u32[]{:S(2)}, u32[]{:S(2)}) async-start(bf16[8,2,32768]{2,1,0:T(2,128)(2,1)} %reshape.298), calls=%async_computation | async-start | bytes 2097152 | tf_op jit(solution)/shard_map/all_to_all | solution.py:69
  157.4 101.4 %reduce-scatter.2.cloned.1.call-start = ((), (), s32[]{:S(2)}) async-start(), calls=%async_computation.3 | async-start | bytes 294912 | tf_op jit(solution)/shard_map/reduce_scatter | solution.py:89
  193.3 1.6 copy-start.4
Sparse Core Ops, SparseCore 0:
  198.0 60.7 reduce-scatter.1
where the time goes:
time: 267 us; the launch traced here: 266 us
  waiting for transfers between devices  71.2 us (27%)
  local copies, waits for them, and re-layouts  71.1 us (27%)
  blocking collectives  63.8 us (24%)
  matrix products  30.3 us (11%)
  between operations  13.8 us (5%)
  starting transfers between devices  11.9 us (4%)
  other arithmetic  3.61 us (1%)
    reduce_scatter x1, waiting for transfers between devices, shards(): lax.psum_scatter(jnp.einsum('kac,kbc->ab', upd_space, ten_space, preferre...  60.9 us
    unnamed x23, local copies, waits for them, and re-layouts  33.5 us
    all_gather x1, blocking collectives, shards(): lax.all_gather(occupied_green, 'ctr', axis=0, tiled=True)  32.9 us
    all_gather x1, blocking collectives, shards(): lax.all_gather(virtual_green, 'ctr', axis=0, tiled=True)  30.9 us
    dot_general x4, matrix products, shards(): jnp.einsum('slm,aslz->asmz', occ_blocks, product, preferred_element_type=...  24.1 us
    all_to_all x1, waiting for transfers between devices, shards(): lax.all_to_all(updated, 'ctr', split_axis=2, concat_axis=0, tiled=True)  10.2 us
    gather x4, local copies, waits for them, and re-layouts, shards(): picked = jnp.take(tensor_rows, jnp.maximum(source_col, 0), axis=1)  8.66 us
    reshape x1, local copies, waits for them, and re-layouts, shards(): accumulated.astype(jnp.bfloat16).reshape(row_count, slot_count, BLK * BLK)  7.84 us
  transfers between devices with their start and end apart: 4, of which 2 were waited for; matrix products, arithmetic and copies ran while one was open for 34% of the time, Pallas kernels for 0%

commit v1 on v0

--- a/solution.py
+++ b/solution.py
@@ -6,6 +6,13 @@
 BLK = 64
 AUXB = 64
 NPR = 8
+
+
+def stacked_exchange(x, axis, split, join):
+    size = lax.axis_size(axis)
+    blocks = jnp.stack(jnp.split(x, size, axis=split), axis=0)
+    blocks = lax.all_to_all(blocks, axis, split_axis=0, concat_axis=0)
+    return jnp.concatenate(blocks, axis=join)
 
 
 def shifted(block, axis, distance):
@@ -66,7 +73,7 @@
         )
     updated = accumulated.astype(jnp.bfloat16).reshape(row_count, slot_count, BLK * BLK)
     upd_region, ten_region = (
-        lax.all_to_all(updated, "ctr", split_axis=2, concat_axis=0, tiled=True),
+        stacked_exchange(updated, "ctr", 2, 0),
         lax.all_to_all(three_centre, "ctr", split_axis=2, concat_axis=0, tiled=True),
     )
     region_rows = upd_region.shape[0]

time: 267 us -> 251 us (0.940)
  local copies, waits for them, and re-layouts: 71.1 us -> 56.2 us
    unnamed x23 -> x30, local copies, waits for them, and re-layouts: 33.5 us -> 25.7 us
    reshape x1, local copies, waits for them, and re-layouts: 7.84 us -> 1.9 us  [shards(): accumulated.astype(jnp.bfloat16).reshape(row_count, slot_count, BLK * BLK)]
    all_to_all x2 -> x1, local copies, waits for them, and re-layouts: 5.47 us -> 0.82 us  [stacked_exchange(): blocks = lax.all_to_all(blocks, axis, split_axis=0, concat_axis=0)]
    convert_element_type x0 -> x1, local copies, waits for them, and re-layouts: none -> 3.07 us  [shards(): accumulated.astype(jnp.bfloat16).reshape(row_count, slot_count, BLK * BLK)]
  transfers between devices with their start and end apart: 4 -> 4, of which waited for: 2 -> 2; matrix products, arithmetic and copies ran while one was open for 34% -> 33% of each run, Pallas kernels for 0% -> 0%
where the time goes in v1:
time: 251 us; the launch traced here: 250 us
  waiting for transfers between devices  71.1 us (28%)
  blocking collectives  63.8 us (25%)
  local copies, waits for them, and re-layouts  56.2 us (22%)
  matrix products  31 us (12%)
  between operations  13.8 us (5%)
  starting transfers between devices  11.7 us (5%)
  other arithmetic  2.71 us (1%)
    reduce_scatter x1, waiting for transfers between devices, shards(): lax.psum_scatter(jnp.einsum('kac,kbc->ab', upd_space, ten_space, preferre...  60.9 us
    all_gather x1, blocking collectives, shards(): lax.all_gather(occupied_green, 'ctr', axis=0, tiled=True)  32.9 us
    all_gather x1, blocking collectives, shards(): lax.all_gather(virtual_green, 'ctr', axis=0, tiled=True)  30.9 us
    unnamed x30, local copies, waits for them, and re-layouts  25.7 us
    dot_general x4, matrix products, shards(): jnp.einsum('slm,aslz->asmz', occ_blocks, product, preferred_element_type=...  24.8 us
    all_to_all x1, waiting for transfers between devices, stacked_exchange(): blocks = lax.all_to_all(blocks, axis, split_axis=0, concat_axis=0)  10.2 us
    gather x4, local copies, waits for them, and re-layouts, shards(): picked = jnp.take(tensor_rows, jnp.maximum(source_col, 0), axis=1)  8.62 us
    all_to_all x1, local copies, waits for them, and re-layouts, shards(): lax.all_to_all(three_centre, 'ctr', split_axis=2, concat_axis=0, tiled=True)  6.13 us
  transfers between devices with their start and end apart: 4, of which 2 were waited for; matrix products, arithmetic and copies ran while one was open for 33% of the time, Pallas kernels for 0%

profile of v1, /device:TPU:0, one launch (start us, length us, event | category | flops | bytes accessed | tf_op | source)
XLA Modules:
  0.0 250.5 jit_solution(1862280302693868501)
XLA Ops:
  6.5 32.9 %all-gather.1 = bf16[8,4,4096]{2,1,0:T(4,128)(2,1)S(1)} all-gather(bf16[1,4,4096]{2,1,0:T(4,128)(2,1)} %bitcast.154), channel_id=1, replica_groups=mesh['dist'=4,'ctr'=8] {'ctr'}, dimensions={0}, use_global_device_ids=true | all-gather | bytes 294912 | tf_op jit(solution)/shard_map/all_gather | solution.py:45
  39.4 30.9 %all-gather = bf16[8,4,4096]{2,1,0:T(4,128)(2,1)S(1)} all-gather(bf16[1,4,4096]{2,1,0:T(4,128)(2,1)} %bitcast.155), channel_id=1, replica_groups=mesh['dist'=4,'ctr'=8] {'ctr'}, dimensions={0}, use_global_device_ids=true | all-gather | bytes 294912 | tf_op jit(solution)/shard_map/all_gather | solution.py:46
  70.5 0.9 pad_maximum_fusion
  71.4 4.8 %copy.36 = bf16[32,4,4096]{0,1,2:T(4,128)(2,1)} copy(bf16[32,4,4096]{2,1,0:T(4,128)(2,1)S(1)} %copy-done.3) | data formatting | bytes 2097152 | tf_op args[0]
  76.2 7.8 %reshape.291 = bf16[8,2,32768]{2,1,0:T(2,128)(2,1)} reshape(bf16[4096,4,32]{2,1,0:T(4,128)(2,1)} %bitcast.149) | data formatting | bytes 2097152
  84.1 5.7 %all-to-all-start.1 = ((bf16[8,2,32768]{2,1,0:T(2,128)(2,1)}), bf16[8,2,32768]{2,1,0:T(2,128)(2,1)}, u32[]{:S(2)}, u32[]{:S(2)}) async-start(bf16[8,2,32768]{2,1,0:T(2,128)(2,1)} %reshape.291), calls=%async_computation.1 | async-start | bytes 2097152 | tf_op jit(solution)/shard_map/all_to_all | solution.py:77
  91.5 0.8 reshape.231
  92.3 1.6 reshape.104
  94.1 2.2 gather_fusion.10
  96.3 2.1 gather_fusion.7
  98.4 2.1 gather_fusion.4
  100.6 2.2 gather_fusion.1
  102.8 1.1 slice_bitcast_fusion
  110.4 6.4 %fusion.2 = f32[4,32,64,64]{3,2,1,0:T(8,128)} fusion(bf16[4,32,64,64]{3,2,1,0:T(8,128)(2,1)} %gather_fusion.7, f32[4]{0:T(128)S(1)} %get-tuple-element.18, pred[4]{0:T(512)(128)(4,1)S(1)} %get-tuple-element.41, bf16[4,64,64]{2,1,0:T(8,128)(2,1)S(1)} %reshape.108, bf16[4,64,64,1]{2,1,0,3:T(8,128)(2,1)S(1)} %reshape.263), kind=kOutput, calls=%fused_computation.19 | convolution fusion | flops 135790592 | bytes 3211284 | tf_op jit(solution)/shard_map/slm,aslz->asmz/dot_general | solution.py:71
  116.8 4.7 %fusion.8 = f32[4,32,64,64]{3,2,1,0:T(8,128)} fusion(bf16[4,32,64,64]{3,2,1,0:T(8,128)(2,1)S(1)} %copy-done.2, f32[4]{0:T(128)S(1)} %get-tuple-element.16, pred[4]{0:T(512)(128)(4,1)S(1)} %get-tuple-element.47, bf16[4,64,64]{2,1,0:T(8,128)(2,1)S(1)} %reshape.103, bf16[4,64,64,1]{2,1,0,3:T(8,128)(2,1)S(1)} %reshape.259), kind=kOutput, calls=%fused_computation.25 | convolution fusion | flops 135790592 | bytes 3211284 | tf_op jit(solution)/shard_map/slm,aslz->asmz/dot_general | solution.py:71
  121.5 6.5 %fusion.5 = f32[4,32,64,64]{3,2,1,0:T(8,128)} fusion(bf16[4,32,64,64]{3,2,1,0:T(8,128)(2,1)} %gather_fusion.4, f32[4]{0:T(128)S(1)} %get-tuple-element.17, pred[4]{0:T(512)(128)(4,1)S(1)} %get-tuple-element.44, bf16[4,64,64]{2,1,0:T(8,128)(2,1)S(1)} %reshape.106, bf16[4,64,64,1]{2,1,0,3:T(8,128)(2,1)S(1)} %reshape.261), kind=kOutput, calls=%fused_computation.22 | convolution fusion | flops 135790592 | bytes 3211284 | tf_op jit(solution)/shard_map/slm,aslz->asmz/dot_general | solution.py:71
  128.0 7.2 %fusion.22 = bf16[32,4,64,64]{2,3,0,1:T(8,128)(2,1)} fusion(f32[4,32,64,64]{3,2,1,0:T(8,128)} %fusion.2, f32[4,32,64,64]{3,2,1,0:T(8,128)} %fusion.8, f32[4,32,64,64]{3,2,1,0:T(8,128)} %fusion.5, bf16[4,32,64,64]{3,2,1,0:T(8,128)(2,1)S(1)} %copy-done.1, f32[4]{0:T(128)S(1)} %get-tuple-element.15, pred[4]{0:T(512)(128)(4,1)S(1)} %get-tuple-element.38, ...), kind=kOutput, calls=%fused_computation.41 | convolution fusion | flops 137887744 | bytes 8454164 | tf_op jit(solution)/shard_map/slm,aslz->asmz/dot_general | solution.py:71
  135.1 3.1 %copy.33 = bf16[32,4,64,64]{3,2,0,1:T(8,128)(2,1)S(1)} copy(bf16[32,4,64,64]{2,3,0,1:T(8,128)(2,1)} %fusion.22) | data formatting | bytes 2097152 | tf_op jit(solution)/shard_map/convert_element_type | solution.py:74
  138.2 1.9 reshape.112
  142.1 0.7 fusion.59
  142.8 0.7 fusion.58
  143.4 0.7 fusion.57
  144.7 0.7 fusion.55
  145.4 6.0 %all-to-all-start = ((bf16[8,32,4,512]{3,1,2,0:T(8,128)(2,1)}), bf16[8,32,4,512]{3,1,2,0:T(8,128)(2,1)S(1)}, u32[]{:S(2)}, u32[]{:S(2)}) async-start(bf16[8,32,4,512]{3,1,2,0:T(8,128)(2,1)} %fusion.55), calls=%async_computation | async-start | bytes 2097152 | tf_op jit(solution)/shard_map/all_to_all | solution.py:14
  151.6 7.0 %reshape.292 = bf16[4096,4,32]{2,1,0:T(4,128)(2,1)} reshape(bf16[8,2,32768]{2,1,0:T(2,128)(2,1)} %all-to-all-done.1) | data formatting | bytes 2097152
  158.7 6.1 %copy.37 = bf16[32,4,8,512]{3,1,0,2:T(4,128)(2,1)S(1)} copy(bf16[32,4,8,512]{0,1,3,2:T(4,128)(2,1)} %bitcast.148) | data formatting | bytes 2097152 | tf_op jit(solution)/shard_map/all_to_all | solution.py:77
  164.8 2.3 convolution_convert_fusion
  167.1 10.2 %all-to-all-done = bf16[8,32,4,512]{3,1,2,0:T(8,128)(2,1)S(1)} async-done(((bf16[8,32,4,512]{3,1,2,0:T(8,128)(2,1)}), bf16[8,32,4,512]{3,1,2,0:T(8,128)(2,1)S(1)}, u32[]{:S(2)}, u32[]{:S(2)}) %all-to-all-start) | async-done | bytes 1048608 | tf_op jit(solution)/shard_map/all_to_all | solution.py:14
  177.3 0.8 copy.34
  178.1 1.0 convolution_convert_fusion.1
  179.7 3.0 %fusion.41 = f32[256,256]{1,0:T(8,128)} fusion(bf16[8,256,512]{2,0,1:T(8,128)(2,1)S(1)} %bitcast.152, bf16[8,256,512]{2,0,1:T(8,128)(2,1)S(1)} %bitcast.153), kind=kOutput, calls=%fused_computation.42 | convolution fusion | flops 536870912 | bytes 4456448 | tf_op jit(solution)/shard_map/kac,kbc->ab/dot_general | solution.py:97
  182.7 60.9 %reduce-scatter.2.cloned.1.call-done = f32[32,256]{1,0:T(8,128)} async-done(((f32[256,256]{1,0:T(8,128)}), f32[32,256]{1,0:T(8,128)}) %reduce-scatter.2.cloned.1.call-update) | async-done | bytes 32784 | tf_op jit(solution)/shard_map/reduce_scatter | solution.py:96
  (90 shorter events, 11.7 us)
Async XLA Ops:
  6.5 83.2 %copy-start = (s32[16,4,4]{0,2,1:T(4,128)S(1)}, s32[16,4,4]{0,2,1:T(4,128)}, u32[]{:S(2)}) copy-start(s32[16,4,4]{0,2,1:T(4,128)} %param.15) | copy-start | bytes 3076
  6.5 64.9 %copy-start.3 = (bf16[32,4,4096]{2,1,0:T(4,128)(2,1)S(1)}, bf16[32,4,4096]{2,1,0:T(4,128)(2,1)}, u32[]{:S(2)}) copy-start(bf16[32,4,4096]{2,1,0:T(4,128)(2,1)} %param.11) | copy-start | bytes 3145732
  71.4 31.4 %collective-permute-start = (bf16[2,32,4096]{2,1,0:T(8,128)(2,1)}, bf16[2,32,4096]{2,1,0:T(8,128)(2,1)}, u32[]{:S(2)}, u32[]{:S(2)}) collective-permute-start(bf16[2,32,4096]{2,1,0:T(8,128)(2,1)} %pad_maximum_fusion), channel_id=1, source_target_pairs={{8,0},{16,8},{24,16},{0,24},{9,1},{17,9},{25,17},{1,25},{10,2},{18... | collective-permute-start | bytes 1572872 | tf_op jit(solution)/shard_map/ppermute | solution.py:21
  84.0 6.3 %copy-start.6 = (s32[16,4,4]{0,2,1:T(4,128)S(1)}, s32[16,4,4]{0,2,1:T(4,128)}, u32[]{:S(2)}) copy-start(s32[16,4,4]{0,2,1:T(4,128)} %param.16) | copy-start | bytes 3076
  84.1 6.8 %copy-start.7 = (s32[16,4,4]{0,2,1:T(4,128)S(1)}, s32[16,4,4]{0,2,1:T(4,128)}, u32[]{:S(2)}) copy-start(s32[16,4,4]{0,2,1:T(4,128)} %param.17) | copy-start | bytes 3076
  84.1 61.4 %all-to-all-start.1 = ((bf16[8,2,32768]{2,1,0:T(2,128)(2,1)}), bf16[8,2,32768]{2,1,0:T(2,128)(2,1)}, u32[]{:S(2)}, u32[]{:S(2)}) async-start(bf16[8,2,32768]{2,1,0:T(2,128)(2,1)} %reshape.291), calls=%async_computation.1 | async-start | bytes 2097152 | tf_op jit(solution)/shard_map/all_to_all | solution.py:77
  100.6 3.3 %copy-start.5 = (bf16[32,4096]{1,0:T(8,128)(2,1)S(1)}, bf16[32,4096]{1,0:T(8,128)(2,1)}, u32[]{:S(2)}) copy-start(bf16[32,4096]{1,0:T(8,128)(2,1)} %reshape.231) | copy-start | bytes 786436
  110.3 6.4 %copy-start.2 = (bf16[4,32,64,64]{3,2,1,0:T(8,128)(2,1)S(1)}, bf16[4,32,64,64]{3,2,1,0:T(8,128)(2,1)}, u32[]{:S(2)}) copy-start(bf16[4,32,64,64]{3,2,1,0:T(8,128)(2,1)} %gather_fusion.1) | copy-start | bytes 3145732
  121.5 6.5 %copy-start.1 = (bf16[4,32,64,64]{3,2,1,0:T(8,128)(2,1)S(1)}, bf16[4,32,64,64]{3,2,1,0:T(8,128)(2,1)}, u32[]{:S(2)}) copy-start(bf16[4,32,64,64]{3,2,1,0:T(8,128)(2,1)} %gather_fusion.10) | copy-start | bytes 3145732
  140.1 11.3 %copy-start.8 = (s32[16,4]{0,1:T(4,128)S(1)}, s32[16,4]{0,1:T(4,128)}, u32[]{:S(2)}) copy-start(s32[16,4]{0,1:T(4,128)} %param.14) | copy-start | bytes 772
  145.4 31.9 %all-to-all-start = ((bf16[8,32,4,512]{3,1,2,0:T(8,128)(2,1)}), bf16[8,32,4,512]{3,1,2,0:T(8,128)(2,1)S(1)}, u32[]{:S(2)}, u32[]{:S(2)}) async-start(bf16[8,32,4,512]{3,1,2,0:T(8,128)(2,1)} %fusion.55), calls=%async_computation | async-start | bytes 2097152 | tf_op jit(solution)/shard_map/all_to_all | solution.py:14
  151.4 92.2 %reduce-scatter.2.cloned.1.call-start = ((), (), s32[]{:S(2)}) async-start(), calls=%async_computation.3 | async-start | bytes 294912 | tf_op jit(solution)/shard_map/reduce_scatter | solution.py:96
  178.1 1.6 copy-start.4
Sparse Core Ops, SparseCore 0:
  182.8 60.7 reduce-scatter.1
